TPU v7x, 512 devices: a whole 4x8x8 slice. The times are simulated.
512 devices in a mesh: row: 32 (over z_hi, y), col: 16 (over z_lo, x, core).
Axes of the slice: x: 4, y: 8, z: 8 (z_hi: 4, z_lo: 2; z = z_hi * 2 + z_lo), core: 2. Of those that a mesh axis runs over, the one named last changes fastest.
Arguments:
- fock: bfloat16 [4096, 4096], P('row', 'col'), may hold values from -0.09375 to 0.09375
- density: bfloat16 [4096, 4096], P('row', 'col'), may hold values from -0.09375 to 0.09375
- intersection: bfloat16 [4096, 4096], P('row', 'col'), may hold values from -6 to 6
- fock_mask: int32 [32, 32], P('row', 'col'), may hold values 0 or 1
- density_mask: int32 [32, 32], P('row', 'col'), may hold values 0 or 1
- intersection_mask: int32 [32, 32], P('row', 'col'), may hold values 0 or 1
- product_filter: int32 [32, 32], P('row', 'col'), may hold values 0 or 1
Outputs:
- residual: float32 [4096, 4096], P('row', 'col')
All inputs are finite; a program needn't handle non-finite values. No bound on the sum of `fock_mask` or of `density_mask` or of `intersection_mask` or of `product_filter` on one device may be relied on, other than what follows from the above.
Results may differ from a plain program's by a relative error of at most 0.0041.
Values may be sent and summed in bfloat16 or wider, within the bound.
A program may use at most 64 MiB of HBM per device.

v0:
```python
import jax
import jax.numpy as jnp
from jax import lax
from jax.experimental import pallas as pl
from jax.experimental.pallas import tpu as pltpu
from jax.sharding import PartitionSpec as P

MESH = pl.DeviceIdType.MESH
Z, Y, J = 4, 8, 4
X = 4
BF16, F32 = jnp.bfloat16, jnp.float32
FAR = F32


def masked(block, mask_ref):
    lane = lax.broadcasted_iota(jnp.int32, block.shape, 1)
    keep = jnp.where(lane < block.shape[1] // 2, mask_ref[0, 0], mask_ref[0, 1])
    return (block.astype(F32) * keep.astype(F32)).astype(BF16)


def kernel(
    f_hbm, p_hbm, s_hbm, fm_hbm, pm_hbm, sm_hbm, filt_hbm, out_ref,
    f_ref, p_ref, s_ref, fm_ref, pm_ref, sm_ref, filt_ref, in_sem,
    f_send, f_all, k_all, p_all, s_all, filt_send, filt_here,
    part, near_in, far_send, far_in, total, part_send, part2_in, own_in, tile_send, tile_in,
    t_send_sem, t_recv_sem,
    p_send_sem, p_recv_sem, p_over_sem, p_core_sem, p_mate_sem,
    s_send_sem, s_recv_sem, s_over_sem, s_core_sem, s_mate_sem,
    f_send_sem, f_recv_sem, k_send_sem, k_recv_sem,
    a_send_sem, a_recv_sem, b_send_sem, b_recv_sem, o_send_sem, o_recv_sem, x_send_sem, x_recv_sem,
):
    r, c = lax.axis_index("row"), lax.axis_index("col")
    zh, y = lax.div(r, Y), lax.rem(r, Y)
    zl, x, core = lax.div(c, 2 * X), lax.rem(lax.div(c, 2), X), lax.rem(c, 2)
    over = (r, c + 1 - 2 * core)
    low = lax.rem(zh, 2)
    pair = zh + 1 - 2 * low
    mate = Z - 1 - zh
    half = lax.rem(lax.div(zh, 2) + low, 2)
    x_high = lax.div(x, 2)
    home = lax.rem(zl + x_high, 2) == half
    away = lax.rem(zl + x_high, 2) != half
    home_row = jnp.where(home, r, pair * Y + y)
    ahead = jnp.where(core == 0, 1, X - 1)

    def holder(l, k):
        return lax.rem(zl + l, 2) * (2 * X) + x * 2 + k

    def slot_of(z_low, at):
        return X * lax.rem(z_low + lax.div(at, 2) + half, 2) + at

    held_z = 2 * lax.div(zh, 2) + core
    held_zl = lax.rem(x_high + half, 2)
    held_l = lax.rem(zl + held_zl, 2)
    held_from = (held_z * Y + y, held_zl * (2 * X) + x * 2 + held_l)
    term_col = held_zl * (2 * X) + x * 2 + core
    move_to = (home_row, holder(core, low))
    stays = jnp.logical_and(home, jnp.logical_and(core == 0, low == 0))
    moved = jnp.logical_not(stays)
    mine = low == core
    not_mine = low != core

    def ring(d):
        return zh * Y + lax.rem(y + d, Y)

    def on_line(dz, dx):
        return lax.rem(zl + dz, 2) * (2 * X) + lax.rem(x + dx, X) * 2 + core

    def tile_to(b):
        return (2 * c + b, lax.div(r, 2))

    def off_diagonal(b):
        return r != 2 * c + b

    def copy(src, dst, send, recv, to):
        return pltpu.make_async_remote_copy(
            src_ref=src, dst_ref=dst, send_sem=send, recv_sem=recv, device_id=to, device_id_type=MESH
        )

    def await_sent(ref, sem):
        copy(ref, ref, sem, sem, over).wait_send()

    def await_recv(ref, sem):
        copy(ref, ref, sem, sem, over).wait_recv()

    fetches = []
    for n, (src, dst) in enumerate((
        (f_hbm, f_ref), (fm_hbm, fm_ref), (p_hbm, p_ref), (pm_hbm, pm_ref),
        (filt_hbm, filt_ref), (s_hbm, s_ref), (sm_hbm, sm_ref),
    )):
        fetches.append(pltpu.make_async_copy(src, dst, in_sem.at[n]))
        fetches[-1].start()

    barrier = pltpu.get_barrier_semaphore()

    def greet(to):
        pl.semaphore_signal(barrier, inc=1, device_id=to, device_id_type=MESH)

    @pl.when(moved)
    def _():
        greet(held_from)

    greet((mate * Y + y, c))
    for d in (2, 6, 1, 7):
        greet((ring(d), c))
    for dz, dx in ((1, 0), (0, 1), (0, X - 1)):
        greet((r, on_line(dz, dx)))
    greet(over)
    greet((pair * Y + y, term_col))

    @pl.when(away)
    def _():
        greet((r, term_col))

    for one in fetches[:5]:
        one.wait()
    f_send[...] = masked(f_ref[...], fm_ref)
    p_all[core, y, low] = masked(p_ref[...], pm_ref)
    lane = lax.broadcasted_iota(jnp.int32, filt_send.shape, 1)
    filt_send[...] = jnp.where(lane < 128, filt_ref[0, 0], filt_ref[0, 1]).astype(F32)

    pl.semaphore_wait(barrier, jnp.where(moved, 1, 0) + 1 + 4 + 3 + 1 + 1 + jnp.where(away, 1, 0))

    my_slot = slot_of(zl, x)
    f_move = copy(f_send, f_all.at[X * core + x], t_send_sem.at[0], t_recv_sem.at[0], move_to)
    filt_move = copy(filt_send, filt_here, t_send_sem.at[1], t_recv_sem.at[1], move_to)

    @pl.when(moved)
    def _():
        f_move.start()
        filt_move.start()

    def mate_copy(buf, sem, t):
        ref = buf.at[core, y, t]
        return copy(ref, ref, sem.at[0], sem.at[1], (mate * Y + y, c))

    def ring_ref(buf, sems, src, t, part_of):
        slot = lax.rem(y + src, Y)
        at = Y + part_of if part_of is not None else slot
        if t is None:
            ref = buf.at[core, slot] if part_of is None else buf.at[core, slot, part_of]
            return ref, sems[1].at[0, at]
        ref = buf.at[core, slot, t] if part_of is None else buf.at[core, slot, t, pl.ds(64 * part_of, 64)]
        return ref, sems[1].at[t, at]

    def ring_send(buf, sems, src, t, d, part_of=None):
        ref, recv = ring_ref(buf, sems, src, t, part_of)
        copy(ref, ref, sems[0], recv, (ring(d), c)).start()

    def ring_wait(buf, sems, src, t, part_of=None):
        await_recv(*ring_ref(buf, sems, src, t, part_of))

    def ring_start(buf, sems, t, to=(2, 6, 1, 7)):
        for d in to:
            ring_send(buf, sems, 0, t, d)

    def ring_pass(buf, sems, t):
        for src, on in ((7, 1), (1, 7)):
            ring_wait(buf, sems, src, t)
            ring_send(buf, sems, src, t, on)

    def ring_relay(buf, sems, t):
        for src, on, far, part_of in ((6, 1, 2, 0), (2, 7, 6, 1)):
            ring_wait(buf, sems, src, t)
            ring_send(buf, sems, src, t, on)
            ring_send(buf, sems, src, t, far, part_of)

    def cross(buf, sems, src):
        at = lax.rem(y + src, Y)
        ref = buf.at[core, at]
        copy(ref, ref, sems[2], sems[3].at[at], over).start()

    def cross_wait(buf, sems, src):
        at = lax.rem(y + src, Y)
        await_recv(buf.at[1 - core, at], sems[3].at[at])

    def ring_last(buf, sems, ts, src):
        for t in ts:
            for part_of in range(2) if src == 4 else (None,):
                ring_wait(buf, sems, src, t, part_of)
        cross(buf, sems, src)

    p_sems = (p_send_sem, p_recv_sem, p_over_sem, p_core_sem)
    s_sems = (s_send_sem, s_recv_sem, s_over_sem, s_core_sem)
    mate_copy(p_all, p_mate_sem, low).start()
    ring_start(p_all, p_sems, low)

    def line_send(buf, sems, dz, dx, to):
        slot = slot_of(lax.rem(zl + dz, 2), lax.rem(x + dx, X))
        ref = buf.at[slot]
        copy(ref, ref, sems[0], sems[1].at[slot], (r, to)).start()

    def line_wait(buf, sems, dz, dx):
        slot = slot_of(lax.rem(zl + dz, 2), lax.rem(x + dx, X))
        await_recv(buf.at[slot], sems[1].at[slot])

    def line_start(buf, sems):
        for to in (on_line(1, 0), on_line(0, ahead), on_line(0, X - ahead)):
            line_send(buf, sems, 0, 0, to)

    def line_relay(buf, sems):
        line_wait(buf, sems, 1, 0)
        line_send(buf, sems, 1, 0, on_line(0, 1))
        line_send(buf, sems, 1, 0, on_line(0, X - 1))
        line_wait(buf, sems, 0, X - ahead)
        line_send(buf, sems, 0, X - ahead, on_line(0, ahead))
        line_send(buf, sems, 0, X - ahead, on_line(1, ahead))

    def line_finish(buf, sems):
        for dz, dx in ((0, ahead), (1, 1), (1, X - 1), (0, 2), (1, 2)):
            line_wait(buf, sems, dz, dx)

    f_sems, k_sems = (f_send_sem, f_recv_sem), (k_send_sem, k_recv_sem)
    mate_copy(p_all, p_mate_sem, 1 - low).wait_recv()
    ring_start(p_all, p_sems, 1 - low)

    @pl.when(moved)
    def _():
        await_recv(f_all.at[my_slot], t_recv_sem.at[0])

    @pl.when(stays)
    def _():
        f_all[my_slot] = f_send[...]

    line_start(f_all, f_sems)
    cross(p_all, p_sems, 0)

    for one in fetches[5:]:
        one.wait()
    s_all[core, y, low] = masked(s_ref[...], sm_ref)
    mate_copy(s_all, s_mate_sem, low).start()

    ring_relay(p_all, p_sems, low)
    line_relay(f_all, f_sems)
    ring_relay(p_all, p_sems, 1 - low)
    cross(p_all, p_sems, 2)
    cross(p_all, p_sems, 6)
    line_finish(f_all, f_sems)

    def at_place(b, src):
        place = lax.rem(y + src, Y)
        j = lax.div(place, 2)
        lanes = pl.ds(pl.multiple_of(128 * lax.rem(place, 2), 128), 128)
        total = None
        for t in range(2):
            rows = f_all[X * lax.rem(j, 2) + 2 * t + lax.div(j, 2), :, lanes]
            term = jnp.dot(rows, p_all[b, place, t], preferred_element_type=F32)
            total = term if total is None else total + term
        return total

    def near_copy():
        return copy(part, near_in, a_send_sem.at[0], a_recv_sem.at[0], (r, holder(1, core)))

    def send_first(b, term):
        @pl.when(away)
        def _():
            far_send[b] = term.astype(FAR)
            copy(
                far_send.at[b], far_in, a_send_sem.at[1], a_recv_sem.at[1], (pair * Y + y, holder(b, core))
            ).start()

        @pl.when(jnp.logical_and(home, b == 0))
        def _():
            near_in[...] = term

        @pl.when(jnp.logical_and(home, b == 1))
        def _():
            part[...] = term
            near_copy().start()

    term = at_place(core, 0) + at_place(core, 2) + at_place(core, 6)
    for src in (1, 7, 5, 3, 4):
        ring_last(p_all, p_sems, (low, 1 - low), src)
        term = term + at_place(core, src)
    mate_copy(s_all, s_mate_sem, 1 - low).wait_recv()
    ring_start(s_all, s_sems, None, (1, 7))
    send_first(core, term)
    cross(s_all, s_sems, 0)

    term = None
    for src in (0, 2, 6, 1, 7, 5, 3, 4):
        cross_wait(p_all, p_sems, src)
        one = at_place(1 - core, src)
        term = one if term is None else term + one
    send_first(1 - core, term)

    @pl.when(moved)
    def _():
        filt_move.wait_recv()

    @pl.when(stays)
    def _():
        filt_here[...] = filt_send[...]

    ring_pass(s_all, s_sems, None)
    cross(s_all, s_sems, 1)
    cross(s_all, s_sems, 7)

    @pl.when(away)
    def _():
        await_recv(near_in, a_recv_sem.at[0])

    await_recv(far_in, a_recv_sem.at[1])
    k_all[my_slot] = ((near_in[...] + far_in[...].astype(F32)) * filt_here[0:1, :]).astype(BF16)
    line_start(k_all, k_sems)
    ring_relay(s_all, s_sems, None)
    line_relay(k_all, k_sems)
    cross(s_all, s_sems, 2)
    cross(s_all, s_sems, 6)
    for src in (5, 3, 4):
        ring_last(s_all, s_sems, (None,), src)
    for src in range(Y):
        cross_wait(s_all, s_sems, src)

    def by_block(dz, dx):
        at = lax.rem(x + dx, X)
        slot = slot_of(lax.rem(zl + dz, 2), at)
        t, j = lax.div(at, 2), 2 * lax.rem(at, 2) + lax.div(slot, X)
        rows = k_all[slot]
        for b in range(2):
            depth = jnp.concatenate([s_all[b, 2 * j, t], s_all[b, 2 * j + 1, t]], axis=0)
            total[b] += jnp.dot(rows, depth, preferred_element_type=F32)

    total[...] = jnp.zeros_like(total)
    for dz, dx in ((0, 0), (1, 0), (0, X - ahead)):
        by_block(dz, dx)
    for dz, dx in ((0, ahead), (1, 1), (1, X - 1), (0, 2), (1, 2)):
        line_wait(k_all, k_sems, dz, dx)
        by_block(dz, dx)

    own_copy = copy(total.at[1 - core], own_in, o_send_sem, o_recv_sem, over)

    @pl.when(mine)
    def _():
        own_copy.start()
        own_in[...] = total[core]

    @pl.when(not_mine)
    def _():
        for b in range(2):
            part_send[b] = total[b].astype(BF16)
            copy(part_send.at[b], part2_in, b_send_sem, b_recv_sem, (pair * Y + y, c - core + b)).start()

    @pl.when(moved)
    def _():
        f_move.wait_send()
        filt_move.wait_send()

    mate_copy(p_all, p_mate_sem, low).wait_send()
    mate_copy(s_all, s_mate_sem, low).wait_send()
    await_sent(p_all.at[0, pl.ds(0, Y - 1)], p_send_sem)
    await_sent(s_all.at[0, pl.ds(0, Y - 1)], s_send_sem)
    await_sent(p_all.at[0], p_over_sem)
    await_sent(s_all.at[0], s_over_sem)
    await_sent(f_all.at[pl.ds(0, 2 * X - 1)], f_send_sem)
    await_sent(k_all.at[pl.ds(0, 2 * X - 1)], k_send_sem)

    @pl.when(away)
    def _():
        await_sent(far_send, a_send_sem.at[1])

    @pl.when(home)
    def _():
        near_copy().wait_send()

    def x_copy(b):
        at = lax.rem(r, 2)
        return copy(tile_send.at[b], tile_in.at[at], x_send_sem.at[b], x_recv_sem.at[at], tile_to(b))

    @pl.when(not_mine)
    def _():
        await_recv(own_in, o_recv_sem)

    await_recv(part2_in, b_recv_sem)
    rounded = (own_in[...] + part2_in[...].astype(F32)).astype(BF16)
    for b in range(2):
        tile_send[b] = rounded[:, 128 * b : 128 * (b + 1)]

        @pl.when(off_diagonal(b))
        def _():
            x_copy(b).start()

        @pl.when(jnp.logical_not(off_diagonal(b)))
        def _():
            tile_in[b] = tile_send[b]

    wide = rounded.astype(F32)

    @pl.when(mine)
    def _():
        own_copy.wait_send()

    @pl.when(not_mine)
    def _():
        await_sent(part_send, b_send_sem)

    for b in range(2):
        here = slice(128 * b, 128 * (b + 1))

        @pl.when(off_diagonal(b))
        def _():
            await_recv(tile_in.at[b], x_recv_sem.at[b])

        out_ref[:, here] = wide[:, here] - tile_in[b].astype(F32).T

    for b in range(2):

        @pl.when(off_diagonal(b))
        def _():
            x_copy(b).wait_send()


def per_device(fock, density, intersection, fock_mask, density_mask, intersection_mask, product_filter):
    hbm = pl.BlockSpec(memory_space=pltpu.HBM)
    vmem = pl.BlockSpec(memory_space=pltpu.VMEM)
    dma = pltpu.SemaphoreType.DMA
    block = (128, 256)
    return pl.pallas_call(
        kernel,
        out_shape=jax.ShapeDtypeStruct(block, F32),
        in_specs=[hbm] * 7,
        out_specs=vmem,
        scratch_shapes=[pltpu.VMEM(block, BF16)] * 3
        + [pltpu.SMEM((1, 2), jnp.int32)] * 4
        + [
            dma((7,)),
            pltpu.VMEM(block, BF16),
            pltpu.VMEM((2 * X,) + block, BF16),
            pltpu.VMEM((2 * X,) + block, BF16),
            pltpu.VMEM((2, Y, 2) + block, BF16),
            pltpu.VMEM((2, Y, 2) + block, BF16),
            pltpu.VMEM((8, 256), F32),
            pltpu.VMEM((8, 256), F32),
            pltpu.VMEM(block, F32),
            pltpu.VMEM(block, F32),
            pltpu.VMEM((2,) + block, FAR),
            pltpu.VMEM(block, FAR),
            pltpu.VMEM((2,) + block, F32),
            pltpu.VMEM((2,) + block, BF16),
            pltpu.VMEM(block, BF16),
            pltpu.VMEM(block, F32),
            pltpu.VMEM((2, 128, 128), BF16),
            pltpu.VMEM((2, 128, 128), BF16),
            dma((2,)), dma((2,)),
            dma, dma((2, Y + 2)), dma, dma((Y,)), dma((2,)),
            dma, dma((2, Y + 2)), dma, dma((Y,)), dma((2,)),
            dma, dma((2 * X,)), dma, dma((2 * X,)),
            dma((2,)), dma((2,)), dma, dma, dma, dma,
            dma((2,)), dma((2,)),
        ],
        compiler_params=pltpu.CompilerParams(
            collective_id=0, has_side_effects=True, vmem_limit_bytes=60 * 1024 * 1024
        ),
        cost_estimate=pl.CostEstimate(flops=2 * 2 * 512 * 1024 * 256, bytes_accessed=6 * 1024 * 1024, transcendentals=0),
    )(fock, density, intersection, fock_mask, density_mask, intersection_mask, product_filter)


def solution(mesh):
    spec = P("row", "col")
    return jax.shard_map(
        per_device, mesh=mesh, in_specs=(spec,) * 7, out_specs=spec, check_vma=False
    )
```

profile of v0, /device:TPU:4, one launch (start us, length us, event | category | flops | bytes accessed | tf_op | source)
XLA Modules:
  0.0 64.0 jit_solution(1695533091843939308)
XLA Ops:
  0.0 62.5 %shard_map.73 = f32[128,256]{1,0:T(8,128)} custom-call(bf16[128,256]{1,0:T(8,128)(2,1)} %f_hbm.1, bf16[128,256]{1,0:T(8,128)(2,1)} %p_hbm.1, bf16[128,256]{1,0:T(8,128)(2,1)} %s_hbm.1, s32[1,2]{1,0:T(1,128)} %fm_hbm.1, s32[1,2]{1,0:T(1,128)} %pm_hbm.1, s32[1,2]{1,0:T(1,128)} %sm_hbm.1, s32[1,2]{1,0:T(1,128)} %filt_hbm.1), custom_call_target="tpu_custom_call" | custom-call | flops 536870912 | bytes 6291456 | tf_op jit(solution)/shard_map/pallas_call | solution.py:418
  62.5 1.6 %copy.9 = f32[128,256]{1,0:T(8,128)} copy(f32[128,256]{1,0:T(8,128)} %shard_map.73) | data formatting | bytes 262144
where the time goes:
time: 64.2 us; the launch traced here: 64 us
  Pallas kernels  62.5 us (97%)
  local copies, waits for them, and re-layouts  1.57 us (2%)
    pallas_call x1, Pallas kernels, per_device(): pl.pallas_call(kernel, out_shape=jax.ShapeDtypeStruct(block, F32), in_spe...  62.5 us
    unnamed x1, local copies, waits for them, and re-layouts  1.57 us

commit v1 on v0

--- a/solution.py
+++ b/solution.py
@@ -235,6 +235,8 @@
     ring_relay(p_all, p_sems, 1 - low)
     cross(p_all, p_sems, 2)
     cross(p_all, p_sems, 6)
+    mate_copy(s_all, s_mate_sem, 1 - low).wait_recv()
+    ring_start(s_all, s_sems, None, (1, 7))
     line_finish(f_all, f_sems)
 
     def at_place(b, src):
@@ -272,10 +274,8 @@
     for src in (1, 7, 5, 3, 4):
         ring_last(p_all, p_sems, (low, 1 - low), src)
         term = term + at_place(core, src)
-    mate_copy(s_all, s_mate_sem, 1 - low).wait_recv()
-    ring_start(s_all, s_sems, None, (1, 7))
     send_first(core, term)
-    cross(s_all, s_sems, 0)
+    ring_pass(s_all, s_sems, None)
 
     term = None
     for src in (0, 2, 6, 1, 7, 5, 3, 4):
@@ -292,9 +292,9 @@
     def _():
         filt_here[...] = filt_send[...]
 
-    ring_pass(s_all, s_sems, None)
-    cross(s_all, s_sems, 1)
-    cross(s_all, s_sems, 7)
+    ring_relay(s_all, s_sems, None)
+    for src in (0, 1, 7, 2, 6):
+        cross(s_all, s_sems, src)
 
     @pl.when(away)
     def _():
@@ -303,10 +303,7 @@
     await_recv(far_in, a_recv_sem.at[1])
     k_all[my_slot] = ((near_in[...] + far_in[...].astype(F32)) * filt_here[0:1, :]).astype(BF16)
     line_start(k_all, k_sems)
-    ring_relay(s_all, s_sems, None)
     line_relay(k_all, k_sems)
-    cross(s_all, s_sems, 2)
-    cross(s_all, s_sems, 6)
     for src in (5, 3, 4):
         ring_last(s_all, s_sems, (None,), src)
     for src in range(Y):

time: 64.2 us -> 62.6 us (0.975)
  the two profiles are of different devices: /device:TPU:4 before, /device:TPU:1 now
where the time goes in v1:
time: 62.6 us; the launch traced here: 61.9 us
  Pallas kernels  60.4 us (96%)
  local copies, waits for them, and re-layouts  1.57 us (3%)
    pallas_call x1, Pallas kernels, per_device(): pl.pallas_call(kernel, out_shape=jax.ShapeDtypeStruct(block, F32), in_spe...  60.4 us
    unnamed x1, local copies, waits for them, and re-layouts  1.57 us

profile of v1, /device:TPU:1, one launch (start us, length us, event | category | flops | bytes accessed | tf_op | source)
XLA Modules:
  0.0 61.9 jit_solution(1130460710743683942)
XLA Ops:
  0.0 60.4 %shard_map.73 = f32[128,256]{1,0:T(8,128)} custom-call(bf16[128,256]{1,0:T(8,128)(2,1)} %f_hbm.1, bf16[128,256]{1,0:T(8,128)(2,1)} %p_hbm.1, bf16[128,256]{1,0:T(8,128)(2,1)} %s_hbm.1, s32[1,2]{1,0:T(1,128)} %fm_hbm.1, s32[1,2]{1,0:T(1,128)} %pm_hbm.1, s32[1,2]{1,0:T(1,128)} %sm_hbm.1, s32[1,2]{1,0:T(1,128)} %filt_hbm.1), custom_call_target="tpu_custom_call" | custom-call | flops 536870912 | bytes 6291456 | tf_op jit(solution)/shard_map/pallas_call | solution.py:415
  60.4 1.6 %copy.9 = f32[128,256]{1,0:T(8,128)} copy(f32[128,256]{1,0:T(8,128)} %shard_map.73) | data formatting | bytes 262144

commit v2 on v1

--- a/solution.py
+++ b/solution.py
@@ -9,7 +9,7 @@
 Z, Y, J = 4, 8, 4
 X = 4
 BF16, F32 = jnp.bfloat16, jnp.float32
-FAR = F32
+FAR = BF16
 
 
 def masked(block, mask_ref):
@@ -408,6 +408,8 @@
 
 
 def per_device(fock, density, intersection, fock_mask, density_mask, intersection_mask, product_filter):
+    operands = fock, density, intersection, fock_mask, density_mask, intersection_mask, product_filter
+    operands = [pltpu.with_memory_space_constraint(one, pltpu.HBM) for one in operands]
     hbm = pl.BlockSpec(memory_space=pltpu.HBM)
     vmem = pl.BlockSpec(memory_space=pltpu.VMEM)
     dma = pltpu.SemaphoreType.DMA
@@ -446,10 +448,10 @@
             dma((2,)), dma((2,)),
         ],
         compiler_params=pltpu.CompilerParams(
-            collective_id=0, has_side_effects=True, vmem_limit_bytes=60 * 1024 * 1024
+            collective_id=0, has_side_effects=True, vmem_limit_bytes=32 * 1024 * 1024
         ),
         cost_estimate=pl.CostEstimate(flops=2 * 2 * 512 * 1024 * 256, bytes_accessed=6 * 1024 * 1024, transcendentals=0),
-    )(fock, density, intersection, fock_mask, density_mask, intersection_mask, product_filter)
+    )(*operands)
 
 
 def solution(mesh):

time: 62.6 us -> 61.7 us (0.986)
  the two profiles are of different devices: /device:TPU:1 before, /device:TPU:65 now
where the time goes in v2:
time: 61.7 us; the launch traced here: 61.5 us
  Pallas kernels  60.9 us (99%)
  local copies, waits for them, and re-layouts  0.66 us (1%)
    pallas_call x1, Pallas kernels, per_device(): pl.pallas_call(kernel, out_shape=jax.ShapeDtypeStruct(block, F32), in_spe...  60.9 us

profile of v2, /device:TPU:65, one launch (start us, length us, event | category | flops | bytes accessed | tf_op | source)
XLA Modules:
  0.0 61.5 jit_solution(10983859841169312957)
XLA Ops:
  0.0 60.9 %shard_map.73 = f32[128,256]{1,0:T(8,128)S(1)} custom-call(bf16[128,256]{1,0:T(8,128)(2,1)} %f_hbm.1, bf16[128,256]{1,0:T(8,128)(2,1)} %p_hbm.1, bf16[128,256]{1,0:T(8,128)(2,1)} %s_hbm.1, s32[1,2]{1,0:T(1,128)} %fm_hbm.1, s32[1,2]{1,0:T(1,128)} %pm_hbm.1, s32[1,2]{1,0:T(1,128)} %sm_hbm.1, s32[1,2]{1,0:T(1,128)} %filt_hbm.1), custom_call_target="tpu_custom_call" | custom-call | flops 536870912 | bytes 6291456 | tf_op jit(solution)/shard_map/pallas_call | solution.py:417
  60.9 0.7 %copy.9 = f32[128,256]{1,0:T(8,128)} copy(f32[128,256]{1,0:T(8,128)S(1)} %shard_map.73) | data formatting | bytes 262144

commit v3 on v2

--- a/solution.py
+++ b/solution.py
@@ -9,7 +9,7 @@
 Z, Y, J = 4, 8, 4
 X = 4
 BF16, F32 = jnp.bfloat16, jnp.float32
-FAR = BF16
+FAR = F32
 
 
 def masked(block, mask_ref):
@@ -101,7 +101,7 @@
         greet(held_from)
 
     greet((mate * Y + y, c))
-    for d in (2, 6, 1, 7):
+    for d in (1, 7):
         greet((ring(d), c))
     for dz, dx in ((1, 0), (0, 1), (0, X - 1)):
         greet((r, on_line(dz, dx)))
@@ -119,7 +119,7 @@
     lane = lax.broadcasted_iota(jnp.int32, filt_send.shape, 1)
     filt_send[...] = jnp.where(lane < 128, filt_ref[0, 0], filt_ref[0, 1]).astype(F32)
 
-    pl.semaphore_wait(barrier, jnp.where(moved, 1, 0) + 1 + 4 + 3 + 1 + 1 + jnp.where(away, 1, 0))
+    pl.semaphore_wait(barrier, jnp.where(moved, 1, 0) + 1 + 2 + 3 + 1 + 1 + jnp.where(away, 1, 0))
 
     my_slot = slot_of(zl, x)
     f_move = copy(f_send, f_all.at[X * core + x], t_send_sem.at[0], t_recv_sem.at[0], move_to)
@@ -150,8 +150,8 @@
     def ring_wait(buf, sems, src, t, part_of=None):
         await_recv(*ring_ref(buf, sems, src, t, part_of))
 
-    def ring_start(buf, sems, t, to=(2, 6, 1, 7)):
-        for d in to:
+    def ring_start(buf, sems, t):
+        for d in (1, 7):
             ring_send(buf, sems, 0, t, d)
 
     def ring_pass(buf, sems, t):
@@ -211,6 +211,7 @@
             line_wait(buf, sems, dz, dx)
 
     f_sems, k_sems = (f_send_sem, f_recv_sem), (k_send_sem, k_recv_sem)
+    ring_pass(p_all, p_sems, low)
     mate_copy(p_all, p_mate_sem, 1 - low).wait_recv()
     ring_start(p_all, p_sems, 1 - low)
 
@@ -232,11 +233,14 @@
 
     ring_relay(p_all, p_sems, low)
     line_relay(f_all, f_sems)
+    ring_pass(p_all, p_sems, 1 - low)
+    cross(p_all, p_sems, 1)
+    cross(p_all, p_sems, 7)
     ring_relay(p_all, p_sems, 1 - low)
     cross(p_all, p_sems, 2)
     cross(p_all, p_sems, 6)
     mate_copy(s_all, s_mate_sem, 1 - low).wait_recv()
-    ring_start(s_all, s_sems, None, (1, 7))
+    ring_start(s_all, s_sems, None)
     line_finish(f_all, f_sems)
 
     def at_place(b, src):
@@ -270,15 +274,17 @@
             part[...] = term
             near_copy().start()
 
-    term = at_place(core, 0) + at_place(core, 2) + at_place(core, 6)
-    for src in (1, 7, 5, 3, 4):
+    term = at_place(core, 0)
+    for src in (1, 7, 2, 6):
+        term = term + at_place(core, src)
+    for src in (5, 3, 4):
         ring_last(p_all, p_sems, (low, 1 - low), src)
         term = term + at_place(core, src)
     send_first(core, term)
     ring_pass(s_all, s_sems, None)
 
     term = None
-    for src in (0, 2, 6, 1, 7, 5, 3, 4):
+    for src in (0, 1, 7, 2, 6, 5, 3, 4):
         cross_wait(p_all, p_sems, src)
         one = at_place(1 - core, src)
         term = one if term is None else term + one

time: 61.7 us -> 66.8 us (1.083)
  the two profiles are of different devices: /device:TPU:65 before, /device:TPU:1 now
where the time goes in v3:
time: 66.8 us; the launch traced here: 66.6 us
  Pallas kernels  65.9 us (99%)
    pallas_call x1, Pallas kernels, per_device(): pl.pallas_call(kernel, out_shape=jax.ShapeDtypeStruct(block, F32), in_spe...  65.9 us

profile of v3, /device:TPU:1, one launch (start us, length us, event | category | flops | bytes accessed | tf_op | source)
XLA Modules:
  0.0 66.6 jit_solution(153374802888960711)
XLA Ops:
  0.0 65.9 %shard_map.73 = f32[128,256]{1,0:T(8,128)S(1)} custom-call(bf16[128,256]{1,0:T(8,128)(2,1)} %f_hbm.1, bf16[128,256]{1,0:T(8,128)(2,1)} %p_hbm.1, bf16[128,256]{1,0:T(8,128)(2,1)} %s_hbm.1, s32[1,2]{1,0:T(1,128)} %fm_hbm.1, s32[1,2]{1,0:T(1,128)} %pm_hbm.1, s32[1,2]{1,0:T(1,128)} %sm_hbm.1, s32[1,2]{1,0:T(1,128)} %filt_hbm.1), custom_call_target="tpu_custom_call" | custom-call | flops 536870912 | bytes 6291456 | tf_op jit(solution)/shard_map/pallas_call | solution.py:423
  65.9 0.7 copy.9

commit v4 on v2

--- a/solution.py
+++ b/solution.py
@@ -22,7 +22,7 @@
     f_hbm, p_hbm, s_hbm, fm_hbm, pm_hbm, sm_hbm, filt_hbm, out_ref,
     f_ref, p_ref, s_ref, fm_ref, pm_ref, sm_ref, filt_ref, in_sem,
     f_send, f_all, k_all, p_all, s_all, filt_send, filt_here,
-    part, near_in, far_send, far_in, total, part_send, part2_in, own_in, tile_send, tile_in,
+    part, near_in, far_send, far_in, total, part_send, part2_in, block_send, block_in, tile_send, tile_in,
     t_send_sem, t_recv_sem,
     p_send_sem, p_recv_sem, p_over_sem, p_core_sem, p_mate_sem,
     s_send_sem, s_recv_sem, s_over_sem, s_core_sem, s_mate_sem,
@@ -58,19 +58,12 @@
     stays = jnp.logical_and(home, jnp.logical_and(core == 0, low == 0))
     moved = jnp.logical_not(stays)
     mine = low == core
-    not_mine = low != core
 
     def ring(d):
         return zh * Y + lax.rem(y + d, Y)
 
     def on_line(dz, dx):
         return lax.rem(zl + dz, 2) * (2 * X) + lax.rem(x + dx, X) * 2 + core
-
-    def tile_to(b):
-        return (2 * c + b, lax.div(r, 2))
-
-    def off_diagonal(b):
-        return r != 2 * c + b
 
     def copy(src, dst, send, recv, to):
         return pltpu.make_async_remote_copy(
@@ -325,18 +318,10 @@
         line_wait(k_all, k_sems, dz, dx)
         by_block(dz, dx)
 
-    own_copy = copy(total.at[1 - core], own_in, o_send_sem, o_recv_sem, over)
-
-    @pl.when(mine)
-    def _():
-        own_copy.start()
-        own_in[...] = total[core]
-
-    @pl.when(not_mine)
-    def _():
-        for b in range(2):
-            part_send[b] = total[b].astype(BF16)
-            copy(part_send.at[b], part2_in, b_send_sem, b_recv_sem, (pair * Y + y, c - core + b)).start()
+    kept_b = jnp.where(mine, 0, 1)
+    part_send[...] = total[1 - kept_b].astype(BF16)
+    part_copy = copy(part_send, part2_in, b_send_sem, b_recv_sem, (pair * Y + y, c))
+    part_copy.start()
 
     @pl.when(moved)
     def _():
@@ -360,51 +345,76 @@
     def _():
         near_copy().wait_send()
 
-    def x_copy(b):
-        at = lax.rem(r, 2)
-        return copy(tile_send.at[b], tile_in.at[at], x_send_sem.at[b], x_recv_sem.at[at], tile_to(b))
-
-    @pl.when(not_mine)
-    def _():
-        await_recv(own_in, o_recv_sem)
-
-    await_recv(part2_in, b_recv_sem)
-    rounded = (own_in[...] + part2_in[...].astype(F32)).astype(BF16)
-    for b in range(2):
-        tile_send[b] = rounded[:, 128 * b : 128 * (b + 1)]
-
-        @pl.when(off_diagonal(b))
-        def _():
-            x_copy(b).start()
-
-        @pl.when(jnp.logical_not(off_diagonal(b)))
-        def _():
-            tile_in[b] = tile_send[b]
-
-    wide = rounded.astype(F32)
-
-    @pl.when(mine)
-    def _():
-        own_copy.wait_send()
-
-    @pl.when(not_mine)
-    def _():
-        await_sent(part_send, b_send_sem)
+    block_row = jnp.where(mine, r, pair * Y + y)
+    block_col = c - core + kept_b
+    own_here = jnp.logical_and(low == 0, core == 0)
+    own_comes = jnp.logical_not(own_here)
+    own_sent = jnp.logical_not(jnp.logical_and(mine, core == 0))
+    block_copy = copy(block_send, block_in, o_send_sem, o_recv_sem, (block_row, block_col))
+
+    def tile_stays(h):
+        return jnp.logical_and(2 * block_col + h == r, lax.div(block_row, 2) == c)
+
+    def tile_copy(h):
+        at = lax.rem(block_row, 2)
+        return copy(
+            tile_send.at[h], tile_in.at[at], x_send_sem.at[h], x_recv_sem.at[at], (2 * block_col + h, lax.div(block_row, 2))
+        )
+
+    def tile_is_here(b):
+        row, col = 2 * c + b, lax.div(r, 2)
+        z = lax.div(row, Y)
+        z_low, second = lax.rem(z, 2), lax.rem(col, 2)
+        z_at = z + second * (1 - 2 * z_low)
+        return jnp.logical_and(z_at * Y + lax.rem(row, Y) == r, col - second + z_low == c)
+
+    part_copy.wait_recv()
+    rounded = (total[kept_b] + part2_in[...].astype(F32)).astype(BF16)
+    for h in range(2):
+        tile_send[h] = rounded[:, 128 * h : 128 * (h + 1)]
+
+        @pl.when(jnp.logical_not(tile_stays(h)))
+        def _():
+            tile_copy(h).start()
+
+        @pl.when(tile_stays(h))
+        def _():
+            tile_in[lax.rem(block_row, 2)] = tile_send[h]
+
+    block_send[...] = rounded
+
+    @pl.when(own_sent)
+    def _():
+        block_copy.start()
+
+    @pl.when(own_here)
+    def _():
+        block_in[...] = rounded
+
+    part_copy.wait_send()
+
+    @pl.when(own_comes)
+    def _():
+        await_recv(block_in, o_recv_sem)
 
     for b in range(2):
         here = slice(128 * b, 128 * (b + 1))
 
-        @pl.when(off_diagonal(b))
+        @pl.when(jnp.logical_not(tile_is_here(b)))
         def _():
             await_recv(tile_in.at[b], x_recv_sem.at[b])
 
-        out_ref[:, here] = wide[:, here] - tile_in[b].astype(F32).T
-
-    for b in range(2):
-
-        @pl.when(off_diagonal(b))
-        def _():
-            x_copy(b).wait_send()
+        out_ref[:, here] = block_in[:, here].astype(F32) - tile_in[b].astype(F32).T
+
+    @pl.when(own_sent)
+    def _():
+        block_copy.wait_send()
+
+    for h in range(2):
+
+        @pl.when(jnp.logical_not(tile_stays(h)))
+        def _():
+            tile_copy(h).wait_send()
 
 
 def per_device(fock, density, intersection, fock_mask, density_mask, intersection_mask, product_filter):
@@ -435,9 +445,10 @@
             pltpu.VMEM((2,) + block, FAR),
             pltpu.VMEM(block, FAR),
             pltpu.VMEM((2,) + block, F32),
-            pltpu.VMEM((2,) + block, BF16),
             pltpu.VMEM(block, BF16),
-            pltpu.VMEM(block, F32),
+            pltpu.VMEM(block, BF16),
+            pltpu.VMEM(block, BF16),
+            pltpu.VMEM(block, BF16),
             pltpu.VMEM((2, 128, 128), BF16),
             pltpu.VMEM((2, 128, 128), BF16),
             dma((2,)), dma((2,)),

time: 61.7 us -> 60.6 us (0.982)
  the two profiles are of different devices: /device:TPU:65 before, /device:TPU:1 now
where the time goes in v4:
time: 60.6 us; the launch traced here: 59.5 us
  Pallas kernels  58.9 us (97%)
  local copies, waits for them, and re-layouts  0.66 us (1%)
    pallas_call x1, Pallas kernels, per_device(): pl.pallas_call(kernel, out_shape=jax.ShapeDtypeStruct(block, F32), in_spe...  58.9 us

profile of v4, /device:TPU:1, one launch (start us, length us, event | category | flops | bytes accessed | tf_op | source)
XLA Modules:
  0.0 59.5 jit_solution(8555745716151326910)
XLA Ops:
  0.0 58.9 %shard_map.73 = f32[128,256]{1,0:T(8,128)S(1)} custom-call(bf16[128,256]{1,0:T(8,128)(2,1)} %f_hbm.1, bf16[128,256]{1,0:T(8,128)(2,1)} %p_hbm.1, bf16[128,256]{1,0:T(8,128)(2,1)} %s_hbm.1, s32[1,2]{1,0:T(1,128)} %fm_hbm.1, s32[1,2]{1,0:T(1,128)} %pm_hbm.1, s32[1,2]{1,0:T(1,128)} %sm_hbm.1, s32[1,2]{1,0:T(1,128)} %filt_hbm.1), custom_call_target="tpu_custom_call" | custom-call | flops 536870912 | bytes 6291456 | tf_op jit(solution)/shard_map/pallas_call | solution.py:427
  58.9 0.7 %copy.9 = f32[128,256]{1,0:T(8,128)} copy(f32[128,256]{1,0:T(8,128)S(1)} %shard_map.73) | data formatting | bytes 262144

commit v5 on v4

--- a/solution.py
+++ b/solution.py
@@ -143,14 +143,9 @@
     def ring_wait(buf, sems, src, t, part_of=None):
         await_recv(*ring_ref(buf, sems, src, t, part_of))
 
-    def ring_start(buf, sems, t, to=(2, 6, 1, 7)):
-        for d in to:
+    def ring_start(buf, sems, t):
+        for d in (2, 6, 1, 7):
             ring_send(buf, sems, 0, t, d)
-
-    def ring_pass(buf, sems, t):
-        for src, on in ((7, 1), (1, 7)):
-            ring_wait(buf, sems, src, t)
-            ring_send(buf, sems, src, t, on)
 
     def ring_relay(buf, sems, t):
         for src, on, far, part_of in ((6, 1, 2, 0), (2, 7, 6, 1)):
@@ -229,7 +224,7 @@
     cross(p_all, p_sems, 2)
     cross(p_all, p_sems, 6)
     mate_copy(s_all, s_mate_sem, 1 - low).wait_recv()
-    ring_start(s_all, s_sems, None, (1, 7))
+    ring_start(s_all, s_sems, None)
     line_finish(f_all, f_sems)
 
     def at_place(b, src):
@@ -268,7 +263,6 @@
         ring_last(p_all, p_sems, (low, 1 - low), src)
         term = term + at_place(core, src)
     send_first(core, term)
-    ring_pass(s_all, s_sems, None)
 
     term = None
     for src in (0, 2, 6, 1, 7, 5, 3, 4):
@@ -286,7 +280,7 @@
         filt_here[...] = filt_send[...]
 
     ring_relay(s_all, s_sems, None)
-    for src in (0, 1, 7, 2, 6):
+    for src in (0, 2, 6):
         cross(s_all, s_sems, src)
 
     @pl.when(away)
@@ -297,7 +291,7 @@
     k_all[my_slot] = ((near_in[...] + far_in[...].astype(F32)) * filt_here[0:1, :]).astype(BF16)
     line_start(k_all, k_sems)
     line_relay(k_all, k_sems)
-    for src in (5, 3, 4):
+    for src in (1, 7, 5, 3, 4):
         ring_last(s_all, s_sems, (None,), src)
     for src in range(Y):
         cross_wait(s_all, s_sems, src)

time: 60.6 us -> 60.9 us (level)
  the two profiles are of different devices: /device:TPU:1 before, /device:TPU:9 now
where the time goes in v5:
time: 60.9 us; the launch traced here: 60.8 us
  Pallas kernels  60.1 us (99%)
  local copies, waits for them, and re-layouts  0.66 us (1%)
    pallas_call x1, Pallas kernels, per_device(): pl.pallas_call(kernel, out_shape=jax.ShapeDtypeStruct(block, F32), in_spe...  60.1 us

profile of v5, /device:TPU:9, one launch (start us, length us, event | category | flops | bytes accessed | tf_op | source)
XLA Modules:
  0.0 60.8 jit_solution(12735838283544126457)
XLA Ops:
  0.0 60.1 %shard_map.73 = f32[128,256]{1,0:T(8,128)S(1)} custom-call(bf16[128,256]{1,0:T(8,128)(2,1)} %f_hbm.1, bf16[128,256]{1,0:T(8,128)(2,1)} %p_hbm.1, bf16[128,256]{1,0:T(8,128)(2,1)} %s_hbm.1, s32[1,2]{1,0:T(1,128)} %fm_hbm.1, s32[1,2]{1,0:T(1,128)} %pm_hbm.1, s32[1,2]{1,0:T(1,128)} %sm_hbm.1, s32[1,2]{1,0:T(1,128)} %filt_hbm.1), custom_call_target="tpu_custom_call" | custom-call | flops 536870912 | bytes 6291456 | tf_op jit(solution)/shard_map/pallas_call | solution.py:421
  60.1 0.7 %copy.9 = f32[128,256]{1,0:T(8,128)} copy(f32[128,256]{1,0:T(8,128)S(1)} %shard_map.73) | data formatting | bytes 262144

commit v6 on v5

--- a/solution.py
+++ b/solution.py
@@ -312,7 +312,8 @@
         line_wait(k_all, k_sems, dz, dx)
         by_block(dz, dx)
 
-    kept_b = jnp.where(mine, 0, 1)
+    odd = lax.rem(y, 2)
+    kept_b = jnp.where(mine, odd, 1 - odd)
     part_send[...] = total[1 - kept_b].astype(BF16)
     part_copy = copy(part_send, part2_in, b_send_sem, b_recv_sem, (pair * Y + y, c))
     part_copy.start()
@@ -341,9 +342,9 @@
 
     block_row = jnp.where(mine, r, pair * Y + y)
     block_col = c - core + kept_b
-    own_here = jnp.logical_and(low == 0, core == 0)
+    own_here = jnp.logical_and(low == core, core == odd)
     own_comes = jnp.logical_not(own_here)
-    own_sent = jnp.logical_not(jnp.logical_and(mine, core == 0))
+    own_sent = own_comes
     block_copy = copy(block_send, block_in, o_send_sem, o_recv_sem, (block_row, block_col))
 
     def tile_stays(h):
@@ -359,7 +360,8 @@
         row, col = 2 * c + b, lax.div(r, 2)
         z = lax.div(row, Y)
         z_low, second = lax.rem(z, 2), lax.rem(col, 2)
-        z_at = z + second * (1 - 2 * z_low)
+        away_by = lax.rem(second + lax.rem(row, 2), 2)
+        z_at = z + away_by * (1 - 2 * z_low)
         return jnp.logical_and(z_at * Y + lax.rem(row, Y) == r, col - second + z_low == c)
 
     part_copy.wait_recv()

time: 60.9 us -> 61.1 us (level)
  the two profiles are of different devices: /device:TPU:9 before, /device:TPU:1 now
where the time goes in v6:
time: 61.1 us; the launch traced here: 61 us
  Pallas kernels  60.3 us (99%)
  local copies, waits for them, and re-layouts  0.66 us (1%)
    pallas_call x1, Pallas kernels, per_device(): pl.pallas_call(kernel, out_shape=jax.ShapeDtypeStruct(block, F32), in_spe...  60.3 us

profile of v6, /device:TPU:1, one launch (start us, length us, event | category | flops | bytes accessed | tf_op | source)
XLA Modules:
  0.0 61.0 jit_solution(4078491710659655206)
XLA Ops:
  0.0 60.3 %shard_map.73 = f32[128,256]{1,0:T(8,128)S(1)} custom-call(bf16[128,256]{1,0:T(8,128)(2,1)} %f_hbm.1, bf16[128,256]{1,0:T(8,128)(2,1)} %p_hbm.1, bf16[128,256]{1,0:T(8,128)(2,1)} %s_hbm.1, s32[1,2]{1,0:T(1,128)} %fm_hbm.1, s32[1,2]{1,0:T(1,128)} %pm_hbm.1, s32[1,2]{1,0:T(1,128)} %sm_hbm.1, s32[1,2]{1,0:T(1,128)} %filt_hbm.1), custom_call_target="tpu_custom_call" | custom-call | flops 536870912 | bytes 6291456 | tf_op jit(solution)/shard_map/pallas_call | solution.py:423
  60.3 0.7 %copy.9 = f32[128,256]{1,0:T(8,128)} copy(f32[128,256]{1,0:T(8,128)S(1)} %shard_map.73) | data formatting | bytes 262144

commit v7 on v5

--- a/solution.py
+++ b/solution.py
@@ -94,6 +94,8 @@
         greet(held_from)
 
     greet((mate * Y + y, c))
+    for d in (2, 6):
+        greet((mate * Y + lax.rem(y + d, Y), c))
     for d in (2, 6, 1, 7):
         greet((ring(d), c))
     for dz, dx in ((1, 0), (0, 1), (0, X - 1)):
@@ -112,7 +114,7 @@
     lane = lax.broadcasted_iota(jnp.int32, filt_send.shape, 1)
     filt_send[...] = jnp.where(lane < 128, filt_ref[0, 0], filt_ref[0, 1]).astype(F32)
 
-    pl.semaphore_wait(barrier, jnp.where(moved, 1, 0) + 1 + 4 + 3 + 1 + 1 + jnp.where(away, 1, 0))
+    pl.semaphore_wait(barrier, jnp.where(moved, 1, 0) + 1 + 2 + 4 + 3 + 1 + 1 + jnp.where(away, 1, 0))
 
     my_slot = slot_of(zl, x)
     f_move = copy(f_send, f_all.at[X * core + x], t_send_sem.at[0], t_recv_sem.at[0], move_to)
@@ -143,8 +145,8 @@
     def ring_wait(buf, sems, src, t, part_of=None):
         await_recv(*ring_ref(buf, sems, src, t, part_of))
 
-    def ring_start(buf, sems, t):
-        for d in (2, 6, 1, 7):
+    def ring_start(buf, sems, t, to=(2, 6, 1, 7)):
+        for d in to:
             ring_send(buf, sems, 0, t, d)
 
     def ring_relay(buf, sems, t):
@@ -171,6 +173,9 @@
     p_sems = (p_send_sem, p_recv_sem, p_over_sem, p_core_sem)
     s_sems = (s_send_sem, s_recv_sem, s_over_sem, s_core_sem)
     mate_copy(p_all, p_mate_sem, low).start()
+    for d in (2, 6):
+        ref, recv = ring_ref(p_all, p_sems, 0, low, None)
+        copy(ref, ref, p_send_sem, recv, (mate * Y + lax.rem(y + d, Y), c)).start()
     ring_start(p_all, p_sems, low)
 
     def line_send(buf, sems, dz, dx, to):
@@ -200,7 +205,7 @@
 
     f_sems, k_sems = (f_send_sem, f_recv_sem), (k_send_sem, k_recv_sem)
     mate_copy(p_all, p_mate_sem, 1 - low).wait_recv()
-    ring_start(p_all, p_sems, 1 - low)
+    ring_start(p_all, p_sems, 1 - low, (1, 7))
 
     @pl.when(moved)
     def _():
@@ -219,8 +224,8 @@
     mate_copy(s_all, s_mate_sem, low).start()
 
     ring_relay(p_all, p_sems, low)
+    ring_relay(p_all, p_sems, 1 - low)
     line_relay(f_all, f_sems)
-    ring_relay(p_all, p_sems, 1 - low)
     cross(p_all, p_sems, 2)
     cross(p_all, p_sems, 6)
     mate_copy(s_all, s_mate_sem, 1 - low).wait_recv()

time: 60.9 us -> 65 us (1.067)
  the two profiles are of different devices: /device:TPU:9 before, /device:TPU:25 now
where the time goes in v7:
time: 65 us; the launch traced here: 64.8 us
  Pallas kernels  64.2 us (99%)
  local copies, waits for them, and re-layouts  0.66 us (1%)
    pallas_call x1, Pallas kernels, per_device(): pl.pallas_call(kernel, out_shape=jax.ShapeDtypeStruct(block, F32), in_spe...  64.2 us

profile of v7, /device:TPU:25, one launch (start us, length us, event | category | flops | bytes accessed | tf_op | source)
XLA Modules:
  0.0 64.8 jit_solution(4900910738219100408)
XLA Ops:
  0.0 64.2 %shard_map.73 = f32[128,256]{1,0:T(8,128)S(1)} custom-call(bf16[128,256]{1,0:T(8,128)(2,1)} %f_hbm.1, bf16[128,256]{1,0:T(8,128)(2,1)} %p_hbm.1, bf16[128,256]{1,0:T(8,128)(2,1)} %s_hbm.1, s32[1,2]{1,0:T(1,128)} %fm_hbm.1, s32[1,2]{1,0:T(1,128)} %pm_hbm.1, s32[1,2]{1,0:T(1,128)} %sm_hbm.1, s32[1,2]{1,0:T(1,128)} %filt_hbm.1), custom_call_target="tpu_custom_call" | custom-call | flops 536870912 | bytes 6291456 | tf_op jit(solution)/shard_map/pallas_call | solution.py:426
  64.2 0.7 %copy.9 = f32[128,256]{1,0:T(8,128)} copy(f32[128,256]{1,0:T(8,128)S(1)} %shard_map.73) | data formatting | bytes 262144

commit v8 on v5

--- a/solution.py
+++ b/solution.py
@@ -199,18 +199,17 @@
             line_wait(buf, sems, dz, dx)
 
     f_sems, k_sems = (f_send_sem, f_recv_sem), (k_send_sem, k_recv_sem)
+    @pl.when(moved)
+    def _():
+        await_recv(f_all.at[my_slot], t_recv_sem.at[0])
+
+    @pl.when(stays)
+    def _():
+        f_all[my_slot] = f_send[...]
+
+    line_start(f_all, f_sems)
     mate_copy(p_all, p_mate_sem, 1 - low).wait_recv()
     ring_start(p_all, p_sems, 1 - low)
-
-    @pl.when(moved)
-    def _():
-        await_recv(f_all.at[my_slot], t_recv_sem.at[0])
-
-    @pl.when(stays)
-    def _():
-        f_all[my_slot] = f_send[...]
-
-    line_start(f_all, f_sems)
     cross(p_all, p_sems, 0)
 
     for one in fetches[5:]:
@@ -218,8 +217,8 @@
     s_all[core, y, low] = masked(s_ref[...], sm_ref)
     mate_copy(s_all, s_mate_sem, low).start()
 
+    line_relay(f_all, f_sems)
     ring_relay(p_all, p_sems, low)
-    line_relay(f_all, f_sems)
     ring_relay(p_all, p_sems, 1 - low)
     cross(p_all, p_sems, 2)
     cross(p_all, p_sems, 6)

time: 60.9 us -> 61.4 us (level)
  the two profiles are of different devices: /device:TPU:9 before, /device:TPU:1 now
where the time goes in v8:
time: 61.4 us; the launch traced here: 61.2 us
  Pallas kernels  60.6 us (99%)
  local copies, waits for them, and re-layouts  0.66 us (1%)
    pallas_call x1, Pallas kernels, per_device(): pl.pallas_call(kernel, out_shape=jax.ShapeDtypeStruct(block, F32), in_spe...  60.6 us

profile of v8, /device:TPU:1, one launch (start us, length us, event | category | flops | bytes accessed | tf_op | source)
XLA Modules:
  0.0 61.2 jit_solution(12002053204601716688)
XLA Ops:
  0.0 60.6 %shard_map.73 = f32[128,256]{1,0:T(8,128)S(1)} custom-call(bf16[128,256]{1,0:T(8,128)(2,1)} %f_hbm.1, bf16[128,256]{1,0:T(8,128)(2,1)} %p_hbm.1, bf16[128,256]{1,0:T(8,128)(2,1)} %s_hbm.1, s32[1,2]{1,0:T(1,128)} %fm_hbm.1, s32[1,2]{1,0:T(1,128)} %pm_hbm.1, s32[1,2]{1,0:T(1,128)} %sm_hbm.1, s32[1,2]{1,0:T(1,128)} %filt_hbm.1), custom_call_target="tpu_custom_call" | custom-call | flops 536870912 | bytes 6291456 | tf_op jit(solution)/shard_map/pallas_call | solution.py:420
  60.6 0.7 %copy.9 = f32[128,256]{1,0:T(8,128)} copy(f32[128,256]{1,0:T(8,128)S(1)} %shard_map.73) | data formatting | bytes 262144

commit v9 on v5

--- a/solution.py
+++ b/solution.py
@@ -9,7 +9,7 @@
 Z, Y, J = 4, 8, 4
 X = 4
 BF16, F32 = jnp.bfloat16, jnp.float32
-FAR = BF16
+FAR = F32
 
 
 def masked(block, mask_ref):
@@ -293,24 +293,30 @@
     line_relay(k_all, k_sems)
     for src in (1, 7, 5, 3, 4):
         ring_last(s_all, s_sems, (None,), src)
-    for src in range(Y):
-        cross_wait(s_all, s_sems, src)
-
-    def by_block(dz, dx):
+
+    def by_block(b, dz, dx):
         at = lax.rem(x + dx, X)
         slot = slot_of(lax.rem(zl + dz, 2), at)
         t, j = lax.div(at, 2), 2 * lax.rem(at, 2) + lax.div(slot, X)
         rows = k_all[slot]
-        for b in range(2):
-            depth = jnp.concatenate([s_all[b, 2 * j, t], s_all[b, 2 * j + 1, t]], axis=0)
-            total[b] += jnp.dot(rows, depth, preferred_element_type=F32)
-
-    total[...] = jnp.zeros_like(total)
-    for dz, dx in ((0, 0), (1, 0), (0, X - ahead)):
-        by_block(dz, dx)
-    for dz, dx in ((0, ahead), (1, 1), (1, X - 1), (0, 2), (1, 2)):
-        line_wait(k_all, k_sems, dz, dx)
-        by_block(dz, dx)
+        depth = jnp.concatenate([s_all[b, 2 * j, t], s_all[b, 2 * j + 1, t]], axis=0)
+        return jnp.dot(rows, depth, preferred_element_type=F32)
+
+    blocks = (0, 0), (1, 0), (0, X - ahead), (0, ahead), (1, 1), (1, X - 1), (0, 2), (1, 2)
+    term = None
+    for n, at in enumerate(blocks):
+        if n >= 3:
+            line_wait(k_all, k_sems, *at)
+        one = by_block(core, *at)
+        term = one if term is None else term + one
+    total[core] = term
+    for src in range(Y):
+        cross_wait(s_all, s_sems, src)
+    term = None
+    for at in blocks:
+        one = by_block(1 - core, *at)
+        term = one if term is None else term + one
+    total[1 - core] = term
 
     kept_b = jnp.where(mine, 0, 1)
     part_send[...] = total[1 - kept_b].astype(BF16)

time: 60.9 us -> 65.3 us (1.072)
  the two profiles are of different devices: /device:TPU:9 before, /device:TPU:1 now
where the time goes in v9:
time: 65.3 us; the launch traced here: 65.2 us
  Pallas kernels  64.5 us (99%)
  local copies, waits for them, and re-layouts  0.66 us (1%)
    pallas_call x1, Pallas kernels, per_device(): pl.pallas_call(kernel, out_shape=jax.ShapeDtypeStruct(block, F32), in_spe...  64.5 us

profile of v9, /device:TPU:1, one launch (start us, length us, event | category | flops | bytes accessed | tf_op | source)
XLA Modules:
  0.0 65.2 jit_solution(14259750011841656225)
XLA Ops:
  0.0 64.5 %shard_map.73 = f32[128,256]{1,0:T(8,128)S(1)} custom-call(bf16[128,256]{1,0:T(8,128)(2,1)} %f_hbm.1, bf16[128,256]{1,0:T(8,128)(2,1)} %p_hbm.1, bf16[128,256]{1,0:T(8,128)(2,1)} %s_hbm.1, s32[1,2]{1,0:T(1,128)} %fm_hbm.1, s32[1,2]{1,0:T(1,128)} %pm_hbm.1, s32[1,2]{1,0:T(1,128)} %sm_hbm.1, s32[1,2]{1,0:T(1,128)} %filt_hbm.1), custom_call_target="tpu_custom_call" | custom-call | flops 536870912 | bytes 6291456 | tf_op jit(solution)/shard_map/pallas_call | solution.py:427
  64.5 0.7 %copy.9 = f32[128,256]{1,0:T(8,128)} copy(f32[128,256]{1,0:T(8,128)S(1)} %shard_map.73) | data formatting | bytes 262144

commit v10 on v9

--- a/solution.py
+++ b/solution.py
@@ -9,7 +9,7 @@
 Z, Y, J = 4, 8, 4
 X = 4
 BF16, F32 = jnp.bfloat16, jnp.float32
-FAR = F32
+FAR = BF16
 
 
 def masked(block, mask_ref):

time: 65.3 us -> 61.2 us (0.937)
  Pallas kernels: 64.5 us -> 60.4 us
    pallas_call x1, Pallas kernels: 64.5 us -> 60.4 us  [per_device(): pl.pallas_call(kernel, out_shape=jax.ShapeDtypeStruct(block, F32), in_spe...]
where the time goes in v10:
time: 61.2 us; the launch traced here: 61.1 us
  Pallas kernels  60.4 us (99%)
  local copies, waits for them, and re-layouts  0.66 us (1%)
    pallas_call x1, Pallas kernels, per_device(): pl.pallas_call(kernel, out_shape=jax.ShapeDtypeStruct(block, F32), in_spe...  60.4 us

profile of v10, /device:TPU:1, one launch (start us, length us, event | category | flops | bytes accessed | tf_op | source)
XLA Modules:
  0.0 61.1 jit_solution(11271265918215959152)
XLA Ops:
  0.0 60.4 %shard_map.73 = f32[128,256]{1,0:T(8,128)S(1)} custom-call(bf16[128,256]{1,0:T(8,128)(2,1)} %f_hbm.1, bf16[128,256]{1,0:T(8,128)(2,1)} %p_hbm.1, bf16[128,256]{1,0:T(8,128)(2,1)} %s_hbm.1, s32[1,2]{1,0:T(1,128)} %fm_hbm.1, s32[1,2]{1,0:T(1,128)} %pm_hbm.1, s32[1,2]{1,0:T(1,128)} %sm_hbm.1, s32[1,2]{1,0:T(1,128)} %filt_hbm.1), custom_call_target="tpu_custom_call" | custom-call | flops 536870912 | bytes 6291456 | tf_op jit(solution)/shard_map/pallas_call | solution.py:427
  60.4 0.7 %copy.9 = f32[128,256]{1,0:T(8,128)} copy(f32[128,256]{1,0:T(8,128)S(1)} %shard_map.73) | data formatting | bytes 262144

commit v11 on v4

--- a/solution.py
+++ b/solution.py
@@ -94,7 +94,7 @@
         greet(held_from)
 
     greet((mate * Y + y, c))
-    for d in (2, 6, 1, 7):
+    for d in (1, 7):
         greet((ring(d), c))
     for dz, dx in ((1, 0), (0, 1), (0, X - 1)):
         greet((r, on_line(dz, dx)))
@@ -112,7 +112,7 @@
     lane = lax.broadcasted_iota(jnp.int32, filt_send.shape, 1)
     filt_send[...] = jnp.where(lane < 128, filt_ref[0, 0], filt_ref[0, 1]).astype(F32)
 
-    pl.semaphore_wait(barrier, jnp.where(moved, 1, 0) + 1 + 4 + 3 + 1 + 1 + jnp.where(away, 1, 0))
+    pl.semaphore_wait(barrier, jnp.where(moved, 1, 0) + 1 + 2 + 3 + 1 + 1 + jnp.where(away, 1, 0))
 
     my_slot = slot_of(zl, x)
     f_move = copy(f_send, f_all.at[X * core + x], t_send_sem.at[0], t_recv_sem.at[0], move_to)
@@ -143,8 +143,8 @@
     def ring_wait(buf, sems, src, t, part_of=None):
         await_recv(*ring_ref(buf, sems, src, t, part_of))
 
-    def ring_start(buf, sems, t, to=(2, 6, 1, 7)):
-        for d in to:
+    def ring_start(buf, sems, t):
+        for d in (1, 7):
             ring_send(buf, sems, 0, t, d)
 
     def ring_pass(buf, sems, t):
@@ -204,6 +204,7 @@
             line_wait(buf, sems, dz, dx)
 
     f_sems, k_sems = (f_send_sem, f_recv_sem), (k_send_sem, k_recv_sem)
+    ring_pass(p_all, p_sems, low)
     mate_copy(p_all, p_mate_sem, 1 - low).wait_recv()
     ring_start(p_all, p_sems, 1 - low)
 
@@ -225,11 +226,14 @@
 
     ring_relay(p_all, p_sems, low)
     line_relay(f_all, f_sems)
+    ring_pass(p_all, p_sems, 1 - low)
+    cross(p_all, p_sems, 1)
+    cross(p_all, p_sems, 7)
     ring_relay(p_all, p_sems, 1 - low)
     cross(p_all, p_sems, 2)
     cross(p_all, p_sems, 6)
     mate_copy(s_all, s_mate_sem, 1 - low).wait_recv()
-    ring_start(s_all, s_sems, None, (1, 7))
+    ring_start(s_all, s_sems, None)
     line_finish(f_all, f_sems)
 
     def at_place(b, src):
@@ -263,15 +267,17 @@
             part[...] = term
             near_copy().start()
 
-    term = at_place(core, 0) + at_place(core, 2) + at_place(core, 6)
-    for src in (1, 7, 5, 3, 4):
+    term = at_place(core, 0)
+    for src in (1, 7, 2, 6):
+        term = term + at_place(core, src)
+    for src in (5, 3, 4):
         ring_last(p_all, p_sems, (low, 1 - low), src)
         term = term + at_place(core, src)
     send_first(core, term)
     ring_pass(s_all, s_sems, None)
 
     term = None
-    for src in (0, 2, 6, 1, 7, 5, 3, 4):
+    for src in (0, 1, 7, 2, 6, 5, 3, 4):
         cross_wait(p_all, p_sems, src)
         one = at_place(1 - core, src)
         term = one if term is None else term + one

time: 60.6 us -> 62.9 us (1.038); the launches traced: 59.5 us -> 62.7 us
  Pallas kernels: 58.9 us -> 62.1 us
    pallas_call x1, Pallas kernels: 58.9 us -> 62.1 us  [per_device(): pl.pallas_call(kernel, out_shape=jax.ShapeDtypeStruct(block, F32), in_spe...]
where the time goes in v11:
time: 62.9 us; the launch traced here: 62.7 us
  Pallas kernels  62.1 us (99%)
  local copies, waits for them, and re-layouts  0.66 us (1%)
    pallas_call x1, Pallas kernels, per_device(): pl.pallas_call(kernel, out_shape=jax.ShapeDtypeStruct(block, F32), in_spe...  62.1 us

profile of v11, /device:TPU:1, one launch (start us, length us, event | category | flops | bytes accessed | tf_op | source)
XLA Modules:
  0.0 62.7 jit_solution(1027978705152831811)
XLA Ops:
  0.0 62.1 %shard_map.73 = f32[128,256]{1,0:T(8,128)S(1)} custom-call(bf16[128,256]{1,0:T(8,128)(2,1)} %f_hbm.1, bf16[128,256]{1,0:T(8,128)(2,1)} %p_hbm.1, bf16[128,256]{1,0:T(8,128)(2,1)} %s_hbm.1, s32[1,2]{1,0:T(1,128)} %fm_hbm.1, s32[1,2]{1,0:T(1,128)} %pm_hbm.1, s32[1,2]{1,0:T(1,128)} %sm_hbm.1, s32[1,2]{1,0:T(1,128)} %filt_hbm.1), custom_call_target="tpu_custom_call" | custom-call | flops 536870912 | bytes 6291456 | tf_op jit(solution)/shard_map/pallas_call | solution.py:433
  62.1 0.7 %copy.9 = f32[128,256]{1,0:T(8,128)} copy(f32[128,256]{1,0:T(8,128)S(1)} %shard_map.73) | data formatting | bytes 262144
